TPU v7x, 32 devices: a whole 2x2x4 slice. The times are simulated.
32 devices in a mesh: cls: 2 (over core), ptcl: 16 (over z, y, x).
Axes of the slice: x: 2, y: 2, z: 4, core: 2. Of those that a mesh axis runs over, the one named last changes fastest.
Arguments:
- particles: bfloat16 [16384, 2048], P('ptcl')
- panels: bfloat16 [2, 128, 2048], P('cls', 'ptcl')
- sigma2: float32 [32], replicated, may hold values from 0.5 to 2
- defocus_bins: int32 [16384], P('ptcl'), may hold values from 0 to 15
- half_sets: int32 [16384], P('ptcl'), may hold values 0 or 1
- prior_mask: int32 [16384, 2], P('ptcl', 'cls'), may hold values from 0 to 1, as said below
- orient_ids: int32 [128], replicated, may hold values from 0 to 127, each once
Outputs:
- half_maps: float32 [2, 256, 2048], P('cls', 'ptcl')
- log_evidence: float32 [16384], P('ptcl')
Inputs may be any that keep to these rules, and one draw needn't show every extreme that they name: `prior_mask`: every particle allows at least one class. `orient_ids`: each direction 0 to 127 appears once.
All inputs are finite; a program needn't handle non-finite values. No bound on the sum of `half_sets` on one device may be relied on, other than what follows from the above.
Results may differ from a plain program's by a relative error of at most 0.0015.
The roundings to bfloat16 on the way count: a program that leaves them out, or rounds other values in their place, can miss the bound.
Values may be sent and summed in bfloat16 or wider, within the bound.
A program may use at most 64 MiB of HBM per device.

v0:
```python
import functools

import jax
import jax.numpy as jnp
import numpy as np
from jax import lax
from jax.experimental import pallas as pl
from jax.experimental.pallas import tpu as pltpu
from jax.sharding import PartitionSpec as P

PIXC = 1024
ORIENT = 128
NSHELL = 32
NBIN = 16
LANES = 128
WIDTH = 2 * PIXC + LANES
TILES = WIDTH // LANES
DATA_TILES = TILES - 1
CHUNKS = ((12, 5), (0, 4), (4, 4), (8, 2), (10, 2))
WINDOW = 2
MESH = pl.DeviceIdType.MESH
BF16 = jnp.bfloat16
F32 = jnp.float32


def ctf_table():
    defocus = (np.arange(NBIN, dtype=np.float32) + np.float32(1.0)) / np.float32(NBIN)
    radius = (np.arange(PIXC, dtype=np.float32) + np.float32(0.5)) / np.float32(PIXC)
    phase = np.float32(0.3) + np.float32(2.5) * defocus[:, None] * radius[None, :]
    wide = phase.astype(np.float64)
    return (np.sin(wide) + 0.1 * np.cos(wide)).astype(np.float32)


def iota(shape, dim):
    return lax.broadcasted_iota(jnp.int32, shape, dim)


def over(values, size):
    return lax.shift_right_logical(values, jnp.int32(size.bit_length() - 1))


def mod(values, size):
    return lax.bitwise_and(values, jnp.int32(size - 1))


def dot(left, right):
    return lax.dot_general(left, right, (((1,), (0,)), ((), ())), preferred_element_type=F32)


def dot_t(left, right):
    return lax.dot_general(left, right, (((1,), (1,)), ((), ())), preferred_element_type=F32)


def split3(values):
    high = values.astype(BF16)
    rest = values - high.astype(F32)
    mid = rest.astype(BF16)
    low = (rest - mid.astype(F32)).astype(BF16)
    return high, mid, low


def exact(values, product):
    high, mid, low = split3(values)
    return product(high) + product(mid) + product(low)


def by_group(values, dim):
    high, mid, low = split3(values)
    axis = [1, 1]
    axis[dim] = values.shape[dim]
    group = over(iota(tuple(axis), dim), NBIN)
    mixed = jnp.where(
        group == 0,
        high.astype(F32),
        jnp.where(group == 1, mid.astype(F32), jnp.where(group == 2, low.astype(F32), 0.0)),
    )
    return mixed.astype(BF16)


def kernel(
    dims,
    particles,
    panels,
    sigma2,
    bins,
    halves,
    prior,
    orient,
    table,
    maps,
    evidence,
    images,
    weighted,
    centred,
    gathered,
    onehot,
    tables,
    noise,
    peaks,
    posts,
    send1,
    recv1,
    acc,
    recv2,
    recv3,
    final,
    swapped,
    shells,
    stats,
    load_sem,
    gsend,
    grecv,
    csend,
    crecv,
    s1send,
    s1recv,
    s2send,
    s2recv,
    xsend,
    xrecv,
    tsend,
    trecv,
):
    n, ncls, plane, line, rows, pad, count = dims
    block = 2 * pad
    total_rows = n * block
    own_rows = line * block
    me = lax.axis_index("ptcl")
    mine = lax.axis_index("cls")
    q = lax.rem(me, plane)
    l = me // plane
    half = me // (n // 2)

    pair = l // 2
    kind = lax.rem(l + pair, 2)

    def line_of(pair_pos, wanted):
        return 2 * pair_pos + lax.rem(pair_pos + wanted, 2)

    def at(line_pos, plane_pos):
        return line_pos * plane + plane_pos

    def remote(src, dst, send, recv, ptcl=None, cls=None):
        return pltpu.make_async_remote_copy(
            src_ref=src,
            dst_ref=dst,
            send_sem=send,
            recv_sem=recv,
            device_id=(mine if cls is None else cls, me if ptcl is None else ptcl),
            device_id_type=MESH,
        )

    barrier = pltpu.get_barrier_semaphore()
    for i in range(1, n):
        pl.semaphore_signal(
            barrier, inc=1, device_id=(mine, lax.rem(me + i, n)), device_id_type=MESH
        )
    for i in range(1, ncls):
        pl.semaphore_signal(
            barrier, inc=1, device_id=(lax.rem(mine + i, ncls), me), device_id_type=MESH
        )
    quarter = count // 4
    loads = []
    for i in range(4):
        span = pl.ds(i * quarter, quarter)
        loads.append(
            pltpu.make_async_copy(particles.at[span], images.at[span], load_sem.at[i])
        )
        loads[-1].start()

    piece = panels[0].astype(F32)
    real, imag = piece[:, :PIXC], piece[:, PIXC:]
    if rows < pad:
        fill = jnp.zeros((pad - rows, PIXC), F32)
        parts = [real, fill, imag, fill]
    else:
        parts = [real, imag]

    def spot(device):
        return gathered.at[pl.ds(pl.multiple_of(device * block, block), block)]

    gathered[pl.ds(pl.multiple_of(me * block, block), block), :] = jnp.concatenate(
        parts, axis=0
    ).astype(BF16)
    pl.semaphore_wait(barrier, n - 1 + ncls - 1)

    sends = []
    line_copies = [None]
    for i in range(1, line):
        copy = remote(
            spot(me), spot(me), gsend.at[i, 0], grecv.at[i, 0], at(lax.rem(l + i, line), q)
        )
        copy.start()
        line_copies.append(copy)
    plane_copies = []

    def forward(i):
        source = at(lax.rem(l + line - i, line), q)
        for p in range(1, plane):
            copy = remote(
                spot(source),
                spot(source),
                gsend.at[i, p],
                grecv.at[i, p],
                at(l, lax.rem(q + p, plane)),
            )
            copy.start()
            plane_copies.append(copy)

    forward(0)

    shell_pick = (iota((LANES, 1), 0) == over(iota((1, PIXC), 1), PIXC // NSHELL)).astype(
        F32
    ).astype(BF16)
    inverse = jnp.broadcast_to(1.0 / sigma2[...], (8, NSHELL))
    noise[...] = exact(inverse, lambda v: dot(v, shell_pick[:NSHELL]))
    base = table[...]
    base = jnp.concatenate(
        [base, base, base, jnp.zeros((LANES - 3 * NBIN, PIXC), F32)], axis=0
    )
    tables[0] = by_group(base, 0)
    tables[1] = (base * base * noise[0:1, :]).astype(BF16)
    tables[2] = (base * base).astype(BF16)
    row = iota((LANES, 1), 0)
    row = jnp.where(row < 3 * NBIN, mod(row, NBIN), -1)
    onehot[...] = (
        jnp.where(row == bins[...], 1.0, 0.0)
    ).astype(BF16)

    step = LANES

    def prepare(first, last):
        def body(i, carry):
            span = pl.ds(pl.multiple_of(i * step, step), step)
            picks = onehot[:, span]
            contrast = lax.dot_general(
                picks, tables[0], (((0,), (0,)), ((), ())), preferred_element_type=F32
            )
            level = noise[0:1, :]
            for part in range(2):
                cols = slice(part * PIXC, (part + 1) * PIXC)
                product = images[span, cols].astype(F32) * contrast
                centred[span, cols] = product.astype(BF16)
                weighted[span, cols] = (product * level).astype(BF16)
            return carry

        lax.fori_loop(first, last, body, 0)

    per = quarter // step
    for i in range(4):
        loads[i].wait()
        for s in range(1, line):
            if min(s, 3) == i:
                line_copies[s].wait_recv()
                forward(s)
        prepare(i * per, (i + 1) * per)

    ids = jnp.broadcast_to(orient[...].astype(F32), (8, ORIENT)).astype(BF16)
    c = iota((1, total_rows), 1)
    c_slot = mod(c, pad)
    c_part = mod(over(c, pad), 2)
    source_id = jnp.where(c_slot < rows, over(c, block) * rows + c_slot, -1)
    expand = jnp.where(source_id == iota((ORIENT, 1), 0), 1.0, 0.0).astype(BF16)
    ids_cols = dot(ids, expand)[0:1, :]
    square = (total_rows, total_rows)
    r = iota((total_rows, 1), 0)
    slot = mod(r, pad)
    r_sub = mod(over(r, block), line)
    r_kind = jnp.where(r_sub < line // 2, kind, 1 - kind)
    r_pair = mod(r_sub + pair, line // 2)
    r_line = 2 * r_pair + mod(r_pair + r_kind, 2)
    r_plane = mod(over(r, own_rows) + q, plane)
    owner = at(r_line, r_plane)
    pairs = n // 2
    direction = mod(owner, pairs) * (2 * rows) + over(owner, pairs) * rows + slot
    direction = jnp.where(slot < rows, direction, -1).astype(F32)
    c_ok = c_slot < rows
    real_ids = jnp.where(c_ok & (c_part == 0), ids_cols, -2.0)
    imag_ids = jnp.where(c_ok & (c_part == 1), ids_cols, -2.0)
    pick_real = jnp.where(jnp.broadcast_to(direction, square) == real_ids, 1.0, 0.0).astype(BF16)
    pick_imag = jnp.where(jnp.broadcast_to(direction, square) == imag_ids, 1.0, 0.0).astype(BF16)
    row_half = mod(over(r, pad), 2)

    for copy in plane_copies:
        copy.wait_recv()
    whole = gathered[...]
    panel_real = dot(pick_real, whole)
    panel_imag = dot(pick_imag, whole)
    panel_power = (panel_real * panel_real + panel_imag * panel_imag).astype(BF16)
    norm = by_group(dot_t(panel_power, tables[1]), 1)
    scores = (
        dot_t(panel_real.astype(BF16), weighted[:, :PIXC])
        + dot_t(panel_imag.astype(BF16), weighted[:, PIXC:])
        - 0.5 * dot(norm, onehot[...])
    )
    use = (prior[...] > 0) & (halves[...] == row_half) & (slot < rows)
    masked = jnp.where(use, scores, -1e30)
    local_peak = jnp.max(masked, axis=0, keepdims=True)
    raw = jnp.where(use, jnp.exp(masked - local_peak), 0.0)
    local_total = jnp.sum(raw, axis=0, keepdims=True)
    peaks[0, 0:1, :] = local_peak
    peaks[0, 1:2, :] = local_total
    class_copies = []
    for i in range(1, ncls):
        copy = remote(
            peaks.at[0],
            peaks.at[i],
            csend.at[i],
            crecv.at[i],
            cls=lax.rem(mine + i, ncls),
        )
        copy.start()
        class_copies.append(copy)
    for copy in class_copies:
        copy.wait_recv()
    peak = local_peak
    for i in range(1, ncls):
        peak = jnp.maximum(peak, peaks[i, 0:1, :])
    total = local_total * jnp.exp(local_peak - peak)
    for i in range(1, ncls):
        total = total + peaks[i, 1:2, :] * jnp.exp(peaks[i, 0:1, :] - peak)
    posts[...] = (raw * (jnp.exp(local_peak - peak) / total)).astype(BF16)
    evidence[...] = peak + jnp.log(total)

    plane_sends, pair_sends, class_sends, swaps = [], [], [], []

    def launch(k):
        first, tiles = CHUNKS[k]
        data_tiles = min(tiles, DATA_TILES - first)
        start = first * LANES
        part = dot(posts[...], centred[:, start : start + data_tiles * LANES])
        for t in range(data_tiles):
            lanes = slice(t * LANES, (t + 1) * LANES)
            for i in range(line):
                acc[i, first + t] = part[i * block : (i + 1) * block, lanes]
            for p in range(1, plane):
                send1[p - 1, first + t] = part[
                    p * own_rows : (p + 1) * own_rows, lanes
                ].astype(BF16)
        if data_tiles < tiles:
            sums = dot_t(posts[...], onehot[...])
            kept = jnp.where(iota((1, LANES), 1) < NBIN, sums[:own_rows], 0.0)
            for i in range(line):
                acc[i, DATA_TILES] = kept[i * block : (i + 1) * block]
            for p in range(1, plane):
                send1[p - 1, DATA_TILES] = by_group(sums[p * own_rows : (p + 1) * own_rows], 1)
        span = pl.ds(first, tiles)
        group = []
        for p in range(1, plane):
            copy = remote(
                send1.at[p - 1, span],
                recv1.at[p - 1, span],
                s1send.at[k, p],
                s1recv.at[k, p],
                at(l, lax.rem(q + p, plane)),
            )
            copy.start()
            group.append(copy)
        plane_sends.append(group)

    def plane_sum(k):
        first, tiles = CHUNKS[k]
        span = pl.ds(first, tiles)
        for copy in plane_sends[k]:
            copy.wait_recv()
        for t in range(first, first + tiles):
            value = recv1[0, t].astype(F32)
            for p in range(2, plane):
                value = value + recv1[p - 1, t].astype(F32)
            for i in range(line):
                acc[i, t] = acc[i, t] + value[i * block : (i + 1) * block]
        copy = remote(
            acc.at[pl.ds(line // 2, line // 2), span],
            recv2.at[:, span],
            s2send.at[k, 0],
            s2recv.at[k, 0],
            at(l + 1 - 2 * lax.rem(l, 2), q),
        )
        copy.start()
        pair_sends.append(copy)

    def pair_sum(k):
        first, tiles = CHUNKS[k]
        span = pl.ds(first, tiles)
        pair_sends[k].wait_recv()
        for i in range(line // 2):
            acc[i, first : first + tiles] = (
                acc[i, first : first + tiles] + recv2[i, first : first + tiles]
            )
        group = []
        for i in range(1, line // 2):
            copy = remote(
                acc.at[i, span],
                recv3.at[i - 1, span],
                s2send.at[k, i],
                s2recv.at[k, i],
                at(line_of(lax.rem(pair + i, line // 2), kind), q),
            )
            copy.start()
            group.append(copy)
        class_sends.append(group)

    def finish(k):
        first, tiles = CHUNKS[k]
        span = pl.ds(first, tiles)
        for copy in class_sends[k]:
            copy.wait_recv()
        for t in range(first, first + tiles):
            value = acc[0, t]
            for i in range(1, line // 2):
                value = value + recv3[i - 1, t]
            zero, one = value[:pad], value[pad:]
            final[0, t] = zero
            final[1, t] = one
            lanes = slice(t * LANES, (t + 1) * LANES)
            for i, product in enumerate((zero * one, zero * zero, one * one)):
                shells[i : i + 1, lanes] = jnp.sum(product, axis=0, keepdims=True)
        copy = remote(
            final.at[1 - half, span],
            swapped.at[half, span],
            xsend.at[k],
            xrecv.at[k],
            lax.rem(me + n // 2, n),
        )
        copy.start()
        swaps.append(copy)

    count_chunks = len(CHUNKS)
    for k in range(WINDOW):
        launch(k)
    for k in range(count_chunks + 2):
        if k < count_chunks:
            plane_sum(k)
        if k + WINDOW < count_chunks:
            launch(k + WINDOW)
        if 1 <= k <= count_chunks:
            pair_sum(k - 1)
        if k >= 2:
            finish(k - 2)

    table_rows = jnp.concatenate(
        [
            shells[0:3, :PIXC] + shells[0:3, PIXC : 2 * PIXC],
            jnp.zeros((5, PIXC), F32),
        ],
        axis=0,
    )
    stats[0] = exact(table_rows, lambda v: dot_t(v, shell_pick))
    stat_copies = []
    for i in range(1, n):
        copy = remote(
            stats.at[0], stats.at[i], tsend.at[i], trecv.at[i], lax.rem(me + i, n)
        )
        copy.start()
        stat_copies.append(copy)
    kept = final[half]
    for copy in swaps:
        copy.wait_recv()
    swapped[half] = kept
    ready = []
    for h in range(2):
        bin_sums = swapped[h, DATA_TILES]
        ready.append(1.0 + exact(bin_sums, lambda v: dot(v, tables[2])))
    for copy in stat_copies:
        copy.wait_recv()
    sums = stats[0]
    for i in range(1, n):
        sums = sums + stats[i]
    fsc = sums[0:1] / jnp.sqrt(sums[1:2] * sums[2:3] + 1e-06)
    factor = jnp.broadcast_to((1.0 + fsc) / 2.0, (8, LANES))
    factor = exact(factor, lambda v: dot(v, shell_pick))[0:1, :]
    for h in range(2):
        scale = factor / ready[h]
        for t in range(DATA_TILES):
            lanes = slice(t * LANES, (t + 1) * LANES)
            k = t % (PIXC // LANES)
            value = swapped[h, t] * scale[:, k * LANES : (k + 1) * LANES]
            maps[0, h * rows : (h + 1) * rows, lanes] = value[:rows]

    for copy in line_copies[1:] + plane_copies + class_copies + stat_copies:
        copy.wait_send()
    for copy in pair_sends + swaps:
        copy.wait_send()
    for group in plane_sends + class_sends:
        for copy in group:
            copy.wait_send()


def write_out(maps, evidence, maps_out, evidence_out):
    maps_out[...] = maps[...]
    evidence_out[...] = evidence[...]


def solution(mesh):
    n = mesh.shape["ptcl"]
    ncls = mesh.shape["cls"]
    plane = 4
    line = n // plane
    rows = ORIENT // n
    pad = max(8, rows)
    block = 2 * pad
    own_rows = line * block
    nchunks = len(CHUNKS)

    def on_device(particles, panels, sigma2, defocus_bins, half_sets, prior_mask, orient_ids):
        count = particles.shape[0]
        dims = (n, ncls, plane, line, rows, pad, count)
        vmem = pl.BlockSpec(memory_space=pltpu.VMEM)
        hbm = pl.BlockSpec(memory_space=pltpu.HBM)
        dma = pltpu.SemaphoreType.DMA
        maps, evidence = pl.pallas_call(
            functools.partial(kernel, dims),
            out_shape=(
                jax.ShapeDtypeStruct((1, 2 * rows, 2 * PIXC), F32),
                jax.ShapeDtypeStruct((1, count), F32),
            ),
            in_specs=[hbm] + [vmem] * 7,
            out_specs=(vmem, vmem),
            scratch_shapes=[
                pltpu.VMEM((count, 2 * PIXC), BF16),
                pltpu.VMEM((count, 2 * PIXC), BF16),
                pltpu.VMEM((count, 2 * PIXC), BF16),
                pltpu.VMEM((n * block, PIXC), BF16),
                pltpu.VMEM((LANES, count), BF16),
                pltpu.VMEM((3, LANES, PIXC), BF16),
                pltpu.VMEM((8, PIXC), F32),
                pltpu.VMEM((ncls, 2, count), F32),
                pltpu.VMEM((n * block, count), BF16),
                pltpu.VMEM((plane - 1, TILES, own_rows, LANES), BF16),
                pltpu.VMEM((plane - 1, TILES, own_rows, LANES), BF16),
                pltpu.VMEM((line, TILES, block, LANES), F32),
                pltpu.VMEM((line // 2, TILES, block, LANES), F32),
                pltpu.VMEM((line // 2 - 1, TILES, block, LANES), F32),
                pltpu.VMEM((2, TILES, pad, LANES), F32),
                pltpu.VMEM((2, TILES, pad, LANES), F32),
                pltpu.VMEM((8, WIDTH), F32),
                pltpu.VMEM((n, 8, LANES), F32),
                dma((4,)),
                dma((line, plane)),
                dma((line, plane)),
                dma((ncls,)),
                dma((ncls,)),
                dma((nchunks, plane)),
                dma((nchunks, plane)),
                dma((nchunks, line)),
                dma((nchunks, line)),
                dma((nchunks,)),
                dma((nchunks,)),
                dma((n,)),
                dma((n,)),
            ],
            compiler_params=pltpu.CompilerParams(
                collective_id=0, has_side_effects=True, vmem_limit_bytes=58 * 2**20
            ),
        )(
            particles,
            panels,
            sigma2.reshape(1, NSHELL),
            defocus_bins.reshape(1, count),
            half_sets.reshape(1, count),
            prior_mask.reshape(1, count),
            orient_ids.reshape(1, ORIENT),
            jnp.asarray(ctf_table()),
        )
        maps, evidence = pl.pallas_call(
            write_out,
            out_shape=(
                jax.ShapeDtypeStruct(maps.shape, F32),
                jax.ShapeDtypeStruct(evidence.shape, F32),
            ),
            in_specs=[vmem, vmem],
            out_specs=(vmem, vmem),
        )(maps, evidence)
        return maps, evidence.reshape(count)

    return jax.shard_map(
        on_device,
        mesh=mesh,
        in_specs=(
            P("ptcl", None),
            P("cls", "ptcl", None),
            P(),
            P("ptcl"),
            P("ptcl"),
            P("ptcl", "cls"),
            P(),
        ),
        out_specs=(P("cls", "ptcl", None), P("ptcl")),
        check_vma=False,
    )
```

profile of v0, /device:TPU:0, one launch (start us, length us, event | category | flops | bytes accessed | tf_op | source)
XLA Modules:
  0.0 51.8 jit_solution(1613206812033153253)
XLA Ops:
  0.6 49.6 %shard_map.95 = (f32[1,16,2048]{2,1,0:T(8,128)}, f32[1,1024]{1,0:T(1,128)}) custom-call(bf16[1024,2048]{1,0:T(8,128)(2,1)} %particles.1, bf16[1,8,2048]{2,1,0:T(8,128)(2,1)} %panels.1, f32[1,32]{1,0:T(1,128)} %bitcast.9, s32[1,1024]{1,0:T(1,128)} %bitcast.6, s32[1,1024]{1,0:T(1,128)} %bitcast.7, s32[1,1024]{1,0:T(1,128)} %bitcast.8, s32[1,128]{1,0:T(1,128)} %bitcast.10, ...), custom_call_target="tpu_custom_call" | custom-call | tf_op jit(solution)/shard_map/pallas_call | solution.py:511
  50.3 1.6 %shard_map.96 = (f32[1,16,2048]{2,1,0:T(8,128)}, f32[1,1024]{1,0:T(1,128)}) custom-call(f32[1,16,2048]{2,1,0:T(8,128)} %get-tuple-element.6.maps, f32[1,1024]{1,0:T(1,128)} %get-tuple-element.7.evidence), custom_call_target="tpu_custom_call" | custom-call | tf_op jit(solution)/shard_map/pallas_call | solution.py:565
where the time goes:
time: 52 us; the launch traced here: 51.8 us
  Pallas kernels  51.2 us (98%)
  between operations  0.64 us (1%)
    pallas_call x1, Pallas kernels, on_device(): pl.pallas_call(functools.partial(kernel, dims), out_shape=(jax.ShapeDtype...  49.6 us
    pallas_call x1, Pallas kernels, on_device(): pl.pallas_call(write_out, out_shape=(jax.ShapeDtypeStruct(maps.shape, F32...  1.57 us

commit v1 on v0

--- a/solution.py
+++ b/solution.py
@@ -17,7 +17,7 @@
 TILES = WIDTH // LANES
 DATA_TILES = TILES - 1
 CHUNKS = ((12, 5), (0, 4), (4, 4), (8, 2), (10, 2))
-WINDOW = 2
+HALVES = 2
 MESH = pl.DeviceIdType.MESH
 BF16 = jnp.bfloat16
 F32 = jnp.float32
@@ -97,6 +97,7 @@
     tables,
     noise,
     peaks,
+    raw,
     posts,
     send1,
     recv1,
@@ -288,39 +289,50 @@
     panel_imag = dot(pick_imag, whole)
     panel_power = (panel_real * panel_real + panel_imag * panel_imag).astype(BF16)
     norm = by_group(dot_t(panel_power, tables[1]), 1)
-    scores = (
-        dot_t(panel_real.astype(BF16), weighted[:, :PIXC])
-        + dot_t(panel_imag.astype(BF16), weighted[:, PIXC:])
-        - 0.5 * dot(norm, onehot[...])
-    )
-    use = (prior[...] > 0) & (halves[...] == row_half) & (slot < rows)
-    masked = jnp.where(use, scores, -1e30)
-    local_peak = jnp.max(masked, axis=0, keepdims=True)
-    raw = jnp.where(use, jnp.exp(masked - local_peak), 0.0)
-    local_total = jnp.sum(raw, axis=0, keepdims=True)
-    peaks[0, 0:1, :] = local_peak
-    peaks[0, 1:2, :] = local_total
+    panel_real = panel_real.astype(BF16)
+    panel_imag = panel_imag.astype(BF16)
+    valid = slot < rows
     class_copies = []
-    for i in range(1, ncls):
-        copy = remote(
-            peaks.at[0],
-            peaks.at[i],
-            csend.at[i],
-            crecv.at[i],
-            cls=lax.rem(mine + i, ncls),
-        )
-        copy.start()
-        class_copies.append(copy)
-    for copy in class_copies:
-        copy.wait_recv()
-    peak = local_peak
-    for i in range(1, ncls):
-        peak = jnp.maximum(peak, peaks[i, 0:1, :])
-    total = local_total * jnp.exp(local_peak - peak)
-    for i in range(1, ncls):
-        total = total + peaks[i, 1:2, :] * jnp.exp(peaks[i, 0:1, :] - peak)
-    posts[...] = (raw * (jnp.exp(local_peak - peak) / total)).astype(BF16)
-    evidence[...] = peak + jnp.log(total)
+    lanes_each = count // HALVES
+    for g in range(HALVES):
+        span = slice(g * lanes_each, (g + 1) * lanes_each)
+        scores = (
+            dot_t(panel_real, weighted[span, :PIXC])
+            + dot_t(panel_imag, weighted[span, PIXC:])
+            - 0.5 * dot(norm, onehot[:, span])
+        )
+        use = (prior[:, span] > 0) & (halves[:, span] == row_half) & valid
+        masked = jnp.where(use, scores, -1e30)
+        local_peak = jnp.max(masked, axis=0, keepdims=True)
+        value = jnp.where(use, jnp.exp(masked - local_peak), 0.0)
+        raw[:, span] = value
+        peaks[0, g, 0:1, :] = local_peak
+        peaks[0, g, 1:2, :] = jnp.sum(value, axis=0, keepdims=True)
+        group = []
+        for i in range(1, ncls):
+            copy = remote(
+                peaks.at[0, g],
+                peaks.at[i, g],
+                csend.at[g, i],
+                crecv.at[g, i],
+                cls=lax.rem(mine + i, ncls),
+            )
+            copy.start()
+            group.append(copy)
+        class_copies.append(group)
+    for g in range(HALVES):
+        span = slice(g * lanes_each, (g + 1) * lanes_each)
+        for copy in class_copies[g]:
+            copy.wait_recv()
+        local_peak = peaks[0, g, 0:1, :]
+        peak = local_peak
+        for i in range(1, ncls):
+            peak = jnp.maximum(peak, peaks[i, g, 0:1, :])
+        total = jnp.zeros_like(peak)
+        for i in range(ncls):
+            total = total + peaks[i, g, 1:2, :] * jnp.exp(peaks[i, g, 0:1, :] - peak)
+        posts[:, span] = (raw[:, span] * (jnp.exp(local_peak - peak) / total)).astype(BF16)
+        evidence[:, span] = peak + jnp.log(total)
 
     plane_sends, pair_sends, class_sends, swaps = [], [], [], []
 
@@ -426,13 +438,11 @@
         swaps.append(copy)
 
     count_chunks = len(CHUNKS)
-    for k in range(WINDOW):
+    for k in range(count_chunks):
         launch(k)
     for k in range(count_chunks + 2):
         if k < count_chunks:
             plane_sum(k)
-        if k + WINDOW < count_chunks:
-            launch(k + WINDOW)
         if 1 <= k <= count_chunks:
             pair_sum(k - 1)
         if k >= 2:
@@ -477,11 +487,11 @@
             value = swapped[h, t] * scale[:, k * LANES : (k + 1) * LANES]
             maps[0, h * rows : (h + 1) * rows, lanes] = value[:rows]
 
-    for copy in line_copies[1:] + plane_copies + class_copies + stat_copies:
+    for copy in line_copies[1:] + plane_copies + stat_copies:
         copy.wait_send()
     for copy in pair_sends + swaps:
         copy.wait_send()
-    for group in plane_sends + class_sends:
+    for group in plane_sends + class_sends + class_copies:
         for copy in group:
             copy.wait_send()
 
@@ -524,7 +534,8 @@
                 pltpu.VMEM((LANES, count), BF16),
                 pltpu.VMEM((3, LANES, PIXC), BF16),
                 pltpu.VMEM((8, PIXC), F32),
-                pltpu.VMEM((ncls, 2, count), F32),
+                pltpu.VMEM((ncls, HALVES, 2, count // HALVES), F32),
+                pltpu.VMEM((n * block, count), F32),
                 pltpu.VMEM((n * block, count), BF16),
                 pltpu.VMEM((plane - 1, TILES, own_rows, LANES), BF16),
                 pltpu.VMEM((plane - 1, TILES, own_rows, LANES), BF16),
@@ -538,8 +549,8 @@
                 dma((4,)),
                 dma((line, plane)),
                 dma((line, plane)),
-                dma((ncls,)),
-                dma((ncls,)),
+                dma((HALVES, ncls)),
+                dma((HALVES, ncls)),
                 dma((nchunks, plane)),
                 dma((nchunks, plane)),
                 dma((nchunks, line)),

time: 52 us -> 52.1 us (level)
  no operation moved by 1% of the time
where the time goes in v1:
time: 52.1 us; the launch traced here: 51.9 us
  Pallas kernels  51.3 us (98%)
  between operations  0.64 us (1%)
    pallas_call x1, Pallas kernels, on_device(): pl.pallas_call(functools.partial(kernel, dims), out_shape=(jax.ShapeDtype...  49.7 us
    pallas_call x1, Pallas kernels, on_device(): pl.pallas_call(write_out, out_shape=(jax.ShapeDtypeStruct(maps.shape, F32...  1.57 us

profile of v1, /device:TPU:0, one launch (start us, length us, event | category | flops | bytes accessed | tf_op | source)
XLA Modules:
  0.0 51.9 jit_solution(2939350043915777401)
XLA Ops:
  0.6 49.7 %shard_map.95 = (f32[1,16,2048]{2,1,0:T(8,128)}, f32[1,1024]{1,0:T(1,128)}) custom-call(bf16[1024,2048]{1,0:T(8,128)(2,1)} %particles.1, bf16[1,8,2048]{2,1,0:T(8,128)(2,1)} %panels.1, f32[1,32]{1,0:T(1,128)} %bitcast.9, s32[1,1024]{1,0:T(1,128)} %bitcast.6, s32[1,1024]{1,0:T(1,128)} %bitcast.7, s32[1,1024]{1,0:T(1,128)} %bitcast.8, s32[1,128]{1,0:T(1,128)} %bitcast.10, ...), custom_call_target="tpu_custom_call" | custom-call | tf_op jit(solution)/shard_map/pallas_call | solution.py:521
  50.4 1.6 %shard_map.96 = (f32[1,16,2048]{2,1,0:T(8,128)}, f32[1,1024]{1,0:T(1,128)}) custom-call(f32[1,16,2048]{2,1,0:T(8,128)} %get-tuple-element.6.maps, f32[1,1024]{1,0:T(1,128)} %get-tuple-element.7.evidence), custom_call_target="tpu_custom_call" | custom-call | tf_op jit(solution)/shard_map/pallas_call | solution.py:576

commit v2 on v1

--- a/solution.py
+++ b/solution.py
@@ -16,7 +16,9 @@
 WIDTH = 2 * PIXC + LANES
 TILES = WIDTH // LANES
 DATA_TILES = TILES - 1
-CHUNKS = ((12, 5), (0, 4), (4, 4), (8, 2), (10, 2))
+CHUNKS = ((12, 5), (0, 4), (4, 4), (8, 4))
+KPARTS = 2
+KWIDTH = PIXC // KPARTS
 HALVES = 2
 MESH = pl.DeviceIdType.MESH
 BF16 = jnp.bfloat16
@@ -103,7 +105,6 @@
     recv1,
     acc,
     recv2,
-    recv3,
     final,
     swapped,
     shells,
@@ -132,12 +133,6 @@
     l = me // plane
     half = me // (n // 2)
 
-    pair = l // 2
-    kind = lax.rem(l + pair, 2)
-
-    def line_of(pair_pos, wanted):
-        return 2 * pair_pos + lax.rem(pair_pos + wanted, 2)
-
     def at(line_pos, plane_pos):
         return line_pos * plane + plane_pos
 
@@ -177,38 +172,44 @@
     else:
         parts = [real, imag]
 
-    def spot(device):
-        return gathered.at[pl.ds(pl.multiple_of(device * block, block), block)]
-
-    gathered[pl.ds(pl.multiple_of(me * block, block), block), :] = jnp.concatenate(
-        parts, axis=0
-    ).astype(BF16)
+    def spot(device, part):
+        return gathered.at[part, pl.ds(pl.multiple_of(device * block, block), block)]
+
+    staged = jnp.concatenate(parts, axis=0).astype(BF16)
+    for part in range(KPARTS):
+        gathered[part, pl.ds(pl.multiple_of(me * block, block), block), :] = staged[
+            :, part * KWIDTH : (part + 1) * KWIDTH
+        ]
     pl.semaphore_wait(barrier, n - 1 + ncls - 1)
 
-    sends = []
-    line_copies = [None]
-    for i in range(1, line):
-        copy = remote(
-            spot(me), spot(me), gsend.at[i, 0], grecv.at[i, 0], at(lax.rem(l + i, line), q)
-        )
-        copy.start()
-        line_copies.append(copy)
-    plane_copies = []
-
-    def forward(i):
+    line_copies = [[None] for _ in range(KPARTS)]
+    plane_copies = [[] for _ in range(KPARTS)]
+
+    def forward(i, part):
         source = at(lax.rem(l + line - i, line), q)
         for p in range(1, plane):
             copy = remote(
-                spot(source),
-                spot(source),
-                gsend.at[i, p],
-                grecv.at[i, p],
+                spot(source, part),
+                spot(source, part),
+                gsend.at[part, i, p],
+                grecv.at[part, i, p],
                 at(l, lax.rem(q + p, plane)),
             )
             copy.start()
-            plane_copies.append(copy)
-
-    forward(0)
+            plane_copies[part].append(copy)
+
+    for part in range(KPARTS):
+        for i in range(1, line):
+            copy = remote(
+                spot(me, part),
+                spot(me, part),
+                gsend.at[part, i, 0],
+                grecv.at[part, i, 0],
+                at(lax.rem(l + i, line), q),
+            )
+            copy.start()
+            line_copies[part].append(copy)
+        forward(0, part)
 
     shell_pick = (iota((LANES, 1), 0) == over(iota((1, PIXC), 1), PIXC // NSHELL)).astype(
         F32
@@ -250,10 +251,10 @@
     per = quarter // step
     for i in range(4):
         loads[i].wait()
-        for s in range(1, line):
-            if min(s, 3) == i:
-                line_copies[s].wait_recv()
-                forward(s)
+        if i in (1, 2):
+            for s in range(1, line):
+                line_copies[i - 1][s].wait_recv()
+                forward(s, i - 1)
         prepare(i * per, (i + 1) * per)
 
     ids = jnp.broadcast_to(orient[...].astype(F32), (8, ORIENT)).astype(BF16)
@@ -267,9 +268,7 @@
     r = iota((total_rows, 1), 0)
     slot = mod(r, pad)
     r_sub = mod(over(r, block), line)
-    r_kind = jnp.where(r_sub < line // 2, kind, 1 - kind)
-    r_pair = mod(r_sub + pair, line // 2)
-    r_line = 2 * r_pair + mod(r_pair + r_kind, 2)
+    r_line = mod(r_sub + l, line)
     r_plane = mod(over(r, own_rows) + q, plane)
     owner = at(r_line, r_plane)
     pairs = n // 2
@@ -282,23 +281,34 @@
     pick_imag = jnp.where(jnp.broadcast_to(direction, square) == imag_ids, 1.0, 0.0).astype(BF16)
     row_half = mod(over(r, pad), 2)
 
-    for copy in plane_copies:
-        copy.wait_recv()
-    whole = gathered[...]
-    panel_real = dot(pick_real, whole)
-    panel_imag = dot(pick_imag, whole)
-    panel_power = (panel_real * panel_real + panel_imag * panel_imag).astype(BF16)
-    norm = by_group(dot_t(panel_power, tables[1]), 1)
-    panel_real = panel_real.astype(BF16)
-    panel_imag = panel_imag.astype(BF16)
+    norm = jnp.zeros((total_rows, LANES), F32)
+    for part in range(KPARTS):
+        for copy in plane_copies[part]:
+            copy.wait_recv()
+        whole = gathered[part]
+        panel_real = dot(pick_real, whole)
+        panel_imag = dot(pick_imag, whole)
+        panel_power = (panel_real * panel_real + panel_imag * panel_imag).astype(BF16)
+        reals = slice(part * KWIDTH, (part + 1) * KWIDTH)
+        imags = slice(PIXC + part * KWIDTH, PIXC + (part + 1) * KWIDTH)
+        norm = norm + dot_t(panel_power, tables[1, :, reals])
+        panel_real = panel_real.astype(BF16)
+        panel_imag = panel_imag.astype(BF16)
+        if part < KPARTS - 1:
+            partial = dot_t(panel_real, weighted[:, reals]) + dot_t(
+                panel_imag, weighted[:, imags]
+            )
+            raw[...] = partial if part == 0 else raw[...] + partial
+    norm = by_group(norm, 1)
     valid = slot < rows
     class_copies = []
     lanes_each = count // HALVES
     for g in range(HALVES):
         span = slice(g * lanes_each, (g + 1) * lanes_each)
         scores = (
-            dot_t(panel_real, weighted[span, :PIXC])
-            + dot_t(panel_imag, weighted[span, PIXC:])
+            raw[:, span]
+            + dot_t(panel_real, weighted[span, reals])
+            + dot_t(panel_imag, weighted[span, imags])
             - 0.5 * dot(norm, onehot[:, span])
         )
         use = (prior[:, span] > 0) & (halves[:, span] == row_half) & valid
@@ -334,7 +344,7 @@
         posts[:, span] = (raw[:, span] * (jnp.exp(local_peak - peak) / total)).astype(BF16)
         evidence[:, span] = peak + jnp.log(total)
 
-    plane_sends, pair_sends, class_sends, swaps = [], [], [], []
+    plane_sends, line_sends, swaps = [], [], []
 
     def launch(k):
         first, tiles = CHUNKS[k]
@@ -381,46 +391,28 @@
                 value = value + recv1[p - 1, t].astype(F32)
             for i in range(line):
                 acc[i, t] = acc[i, t] + value[i * block : (i + 1) * block]
-        copy = remote(
-            acc.at[pl.ds(line // 2, line // 2), span],
-            recv2.at[:, span],
-            s2send.at[k, 0],
-            s2recv.at[k, 0],
-            at(l + 1 - 2 * lax.rem(l, 2), q),
-        )
-        copy.start()
-        pair_sends.append(copy)
-
-    def pair_sum(k):
-        first, tiles = CHUNKS[k]
-        span = pl.ds(first, tiles)
-        pair_sends[k].wait_recv()
-        for i in range(line // 2):
-            acc[i, first : first + tiles] = (
-                acc[i, first : first + tiles] + recv2[i, first : first + tiles]
-            )
         group = []
-        for i in range(1, line // 2):
+        for i in range(1, line):
             copy = remote(
                 acc.at[i, span],
-                recv3.at[i - 1, span],
+                recv2.at[i - 1, span],
                 s2send.at[k, i],
                 s2recv.at[k, i],
-                at(line_of(lax.rem(pair + i, line // 2), kind), q),
+                at(lax.rem(l + i, line), q),
             )
             copy.start()
             group.append(copy)
-        class_sends.append(group)
+        line_sends.append(group)
 
     def finish(k):
         first, tiles = CHUNKS[k]
         span = pl.ds(first, tiles)
-        for copy in class_sends[k]:
+        for copy in line_sends[k]:
             copy.wait_recv()
         for t in range(first, first + tiles):
             value = acc[0, t]
-            for i in range(1, line // 2):
-                value = value + recv3[i - 1, t]
+            for i in range(1, line):
+                value = value + recv2[i - 1, t]
             zero, one = value[:pad], value[pad:]
             final[0, t] = zero
             final[1, t] = one
@@ -440,13 +432,11 @@
     count_chunks = len(CHUNKS)
     for k in range(count_chunks):
         launch(k)
-    for k in range(count_chunks + 2):
+    for k in range(count_chunks + 1):
         if k < count_chunks:
             plane_sum(k)
-        if 1 <= k <= count_chunks:
-            pair_sum(k - 1)
-        if k >= 2:
-            finish(k - 2)
+        if k >= 1:
+            finish(k - 1)
 
     table_rows = jnp.concatenate(
         [
@@ -487,11 +477,14 @@
             value = swapped[h, t] * scale[:, k * LANES : (k + 1) * LANES]
             maps[0, h * rows : (h + 1) * rows, lanes] = value[:rows]
 
-    for copy in line_copies[1:] + plane_copies + stat_copies:
+    for part in range(KPARTS):
+        for copy in line_copies[part][1:] + plane_copies[part]:
+            copy.wait_send()
+    for copy in stat_copies:
         copy.wait_send()
-    for copy in pair_sends + swaps:
+    for copy in swaps:
         copy.wait_send()
-    for group in plane_sends + class_sends + class_copies:
+    for group in plane_sends + line_sends + class_copies:
         for copy in group:
             copy.wait_send()
 
@@ -530,7 +523,7 @@
                 pltpu.VMEM((count, 2 * PIXC), BF16),
                 pltpu.VMEM((count, 2 * PIXC), BF16),
                 pltpu.VMEM((count, 2 * PIXC), BF16),
-                pltpu.VMEM((n * block, PIXC), BF16),
+                pltpu.VMEM((KPARTS, n * block, KWIDTH), BF16),
                 pltpu.VMEM((LANES, count), BF16),
                 pltpu.VMEM((3, LANES, PIXC), BF16),
                 pltpu.VMEM((8, PIXC), F32),
@@ -540,15 +533,14 @@
                 pltpu.VMEM((plane - 1, TILES, own_rows, LANES), BF16),
                 pltpu.VMEM((plane - 1, TILES, own_rows, LANES), BF16),
                 pltpu.VMEM((line, TILES, block, LANES), F32),
-                pltpu.VMEM((line // 2, TILES, block, LANES), F32),
-                pltpu.VMEM((line // 2 - 1, TILES, block, LANES), F32),
+                pltpu.VMEM((line - 1, TILES, block, LANES), F32),
                 pltpu.VMEM((2, TILES, pad, LANES), F32),
                 pltpu.VMEM((2, TILES, pad, LANES), F32),
                 pltpu.VMEM((8, WIDTH), F32),
                 pltpu.VMEM((n, 8, LANES), F32),
                 dma((4,)),
-                dma((line, plane)),
-                dma((line, plane)),
+                dma((KPARTS, line, plane)),
+                dma((KPARTS, line, plane)),
                 dma((HALVES, ncls)),
                 dma((HALVES, ncls)),
                 dma((nchunks, plane)),

time: 52.1 us -> 50.6 us (0.971)
  Pallas kernels: 51.3 us -> 49.8 us
    pallas_call x1, Pallas kernels: 49.7 us -> 48.2 us  [on_device(): pl.pallas_call(functools.partial(kernel, dims), out_shape=(jax.ShapeDtype...]
where the time goes in v2:
time: 50.6 us; the launch traced here: 50.4 us
  Pallas kernels  49.8 us (98%)
  between operations  0.64 us (1%)
    pallas_call x1, Pallas kernels, on_device(): pl.pallas_call(functools.partial(kernel, dims), out_shape=(jax.ShapeDtype...  48.2 us
    pallas_call x1, Pallas kernels, on_device(): pl.pallas_call(write_out, out_shape=(jax.ShapeDtypeStruct(maps.shape, F32...  1.57 us

profile of v2, /device:TPU:0, one launch (start us, length us, event | category | flops | bytes accessed | tf_op | source)
XLA Modules:
  0.0 50.4 jit_solution(15952236856033960071)
XLA Ops:
  0.6 48.2 %shard_map.95 = (f32[1,16,2048]{2,1,0:T(8,128)}, f32[1,1024]{1,0:T(1,128)}) custom-call(bf16[1024,2048]{1,0:T(8,128)(2,1)} %particles.1, bf16[1,8,2048]{2,1,0:T(8,128)(2,1)} %panels.1, f32[1,32]{1,0:T(1,128)} %bitcast.9, s32[1,1024]{1,0:T(1,128)} %bitcast.6, s32[1,1024]{1,0:T(1,128)} %bitcast.7, s32[1,1024]{1,0:T(1,128)} %bitcast.8, s32[1,128]{1,0:T(1,128)} %bitcast.10, ...), custom_call_target="tpu_custom_call" | custom-call | tf_op jit(solution)/shard_map/pallas_call | solution.py:514
  48.9 1.6 %shard_map.96 = (f32[1,16,2048]{2,1,0:T(8,128)}, f32[1,1024]{1,0:T(1,128)}) custom-call(f32[1,16,2048]{2,1,0:T(8,128)} %get-tuple-element.6.maps, f32[1,1024]{1,0:T(1,128)} %get-tuple-element.7.evidence), custom_call_target="tpu_custom_call" | custom-call | tf_op jit(solution)/shard_map/pallas_call | solution.py:568

commit v3 on v2

--- a/solution.py
+++ b/solution.py
@@ -103,6 +103,7 @@
     posts,
     send1,
     recv1,
+    held,
     acc,
     recv2,
     final,
@@ -269,7 +270,7 @@
     slot = mod(r, pad)
     r_sub = mod(over(r, block), line)
     r_line = mod(r_sub + l, line)
-    r_plane = mod(over(r, own_rows) + q, plane)
+    r_plane = lax.bitwise_xor(over(r, own_rows), q)
     owner = at(r_line, r_plane)
     pairs = n // 2
     direction = mod(owner, pairs) * (2 * rows) + over(owner, pairs) * rows + slot
@@ -346,49 +347,74 @@
 
     plane_sends, line_sends, swaps = [], [], []
 
+    def ways(k):
+        return (1, 2) if k % 2 == 0 else (2, 1)
+
+    def across(b):
+        return lax.rem(lax.rem(q, 2) + b % 2, 2) + 2 * lax.rem(q // 2 + b // 2, 2)
+
     def launch(k):
         first, tiles = CHUNKS[k]
         data_tiles = min(tiles, DATA_TILES - first)
+        near, far = ways(k)
         start = first * LANES
         part = dot(posts[...], centred[:, start : start + data_tiles * LANES])
         for t in range(data_tiles):
             lanes = slice(t * LANES, (t + 1) * LANES)
             for i in range(line):
                 acc[i, first + t] = part[i * block : (i + 1) * block, lanes]
-            for p in range(1, plane):
+            for p in (near, 3):
                 send1[p - 1, first + t] = part[
                     p * own_rows : (p + 1) * own_rows, lanes
                 ].astype(BF16)
+            held[first + t] = part[far * own_rows : (far + 1) * own_rows, lanes]
         if data_tiles < tiles:
             sums = dot_t(posts[...], onehot[...])
-            kept = jnp.where(iota((1, LANES), 1) < NBIN, sums[:own_rows], 0.0)
+            kept = jnp.where(iota((1, LANES), 1) < NBIN, sums, 0.0)
+            held[DATA_TILES] = kept[far * own_rows : (far + 1) * own_rows]
             for i in range(line):
                 acc[i, DATA_TILES] = kept[i * block : (i + 1) * block]
-            for p in range(1, plane):
+            for p in (near, 3):
                 send1[p - 1, DATA_TILES] = by_group(sums[p * own_rows : (p + 1) * own_rows], 1)
         span = pl.ds(first, tiles)
+        near, far = ways(k)
         group = []
-        for p in range(1, plane):
+        for b in (3, near):
             copy = remote(
-                send1.at[p - 1, span],
-                recv1.at[p - 1, span],
-                s1send.at[k, p],
-                s1recv.at[k, p],
-                at(l, lax.rem(q + p, plane)),
+                send1.at[b - 1, span],
+                recv1.at[b - 1, span],
+                s1send.at[k, b],
+                s1recv.at[k, b],
+                at(l, across(near)),
             )
             copy.start()
             group.append(copy)
         plane_sends.append(group)
 
+    def relay(k):
+        first, tiles = CHUNKS[k]
+        span = pl.ds(first, tiles)
+        near, far = ways(k)
+        plane_sends[k][0].wait_recv()
+        for t in range(first, first + tiles):
+            send1[far - 1, t] = (held[t] + recv1[2, t].astype(F32)).astype(BF16)
+        copy = remote(
+            send1.at[far - 1, span],
+            recv1.at[far - 1, span],
+            s1send.at[k, far],
+            s1recv.at[k, far],
+            at(l, across(far)),
+        )
+        copy.start()
+        plane_sends[k].append(copy)
+
     def plane_sum(k):
         first, tiles = CHUNKS[k]
         span = pl.ds(first, tiles)
-        for copy in plane_sends[k]:
-            copy.wait_recv()
+        plane_sends[k][1].wait_recv()
+        plane_sends[k][2].wait_recv()
         for t in range(first, first + tiles):
-            value = recv1[0, t].astype(F32)
-            for p in range(2, plane):
-                value = value + recv1[p - 1, t].astype(F32)
+            value = recv1[0, t].astype(F32) + recv1[1, t].astype(F32)
             for i in range(line):
                 acc[i, t] = acc[i, t] + value[i * block : (i + 1) * block]
         group = []
@@ -432,11 +458,13 @@
     count_chunks = len(CHUNKS)
     for k in range(count_chunks):
         launch(k)
-    for k in range(count_chunks + 1):
+    for k in range(count_chunks + 2):
         if k < count_chunks:
-            plane_sum(k)
-        if k >= 1:
-            finish(k - 1)
+            relay(k)
+        if 1 <= k <= count_chunks:
+            plane_sum(k - 1)
+        if k >= 2:
+            finish(k - 2)
 
     table_rows = jnp.concatenate(
         [
@@ -532,6 +560,7 @@
                 pltpu.VMEM((n * block, count), BF16),
                 pltpu.VMEM((plane - 1, TILES, own_rows, LANES), BF16),
                 pltpu.VMEM((plane - 1, TILES, own_rows, LANES), BF16),
+                pltpu.VMEM((TILES, own_rows, LANES), F32),
                 pltpu.VMEM((line, TILES, block, LANES), F32),
                 pltpu.VMEM((line - 1, TILES, block, LANES), F32),
                 pltpu.VMEM((2, TILES, pad, LANES), F32),

time: 50.6 us -> 55.2 us (1.091)
  Pallas kernels: 49.8 us -> 54.4 us
    pallas_call x1, Pallas kernels: 48.2 us -> 52.8 us  [on_device(): pl.pallas_call(functools.partial(kernel, dims), out_shape=(jax.ShapeDtype...]
where the time goes in v3:
time: 55.2 us; the launch traced here: 55 us
  Pallas kernels  54.4 us (99%)
  between operations  0.64 us (1%)
    pallas_call x1, Pallas kernels, on_device(): pl.pallas_call(functools.partial(kernel, dims), out_shape=(jax.ShapeDtype...  52.8 us
    pallas_call x1, Pallas kernels, on_device(): pl.pallas_call(write_out, out_shape=(jax.ShapeDtypeStruct(maps.shape, F32...  1.57 us

profile of v3, /device:TPU:0, one launch (start us, length us, event | category | flops | bytes accessed | tf_op | source)
XLA Modules:
  0.0 55.0 jit_solution(3787696791796134232)
XLA Ops:
  0.6 52.8 %shard_map.95 = (f32[1,16,2048]{2,1,0:T(8,128)}, f32[1,1024]{1,0:T(1,128)}) custom-call(bf16[1024,2048]{1,0:T(8,128)(2,1)} %particles.1, bf16[1,8,2048]{2,1,0:T(8,128)(2,1)} %panels.1, f32[1,32]{1,0:T(1,128)} %bitcast.9, s32[1,1024]{1,0:T(1,128)} %bitcast.6, s32[1,1024]{1,0:T(1,128)} %bitcast.7, s32[1,1024]{1,0:T(1,128)} %bitcast.8, s32[1,128]{1,0:T(1,128)} %bitcast.10, ...), custom_call_target="tpu_custom_call" | custom-call | tf_op jit(solution)/shard_map/pallas_call | solution.py:542
  53.5 1.6 %shard_map.96 = (f32[1,16,2048]{2,1,0:T(8,128)}, f32[1,1024]{1,0:T(1,128)}) custom-call(f32[1,16,2048]{2,1,0:T(8,128)} %get-tuple-element.6.maps, f32[1,1024]{1,0:T(1,128)} %get-tuple-element.7.evidence), custom_call_target="tpu_custom_call" | custom-call | tf_op jit(solution)/shard_map/pallas_call | solution.py:597

commit v4 on v2

--- a/solution.py
+++ b/solution.py
@@ -182,34 +182,21 @@
         ]
     pl.semaphore_wait(barrier, n - 1 + ncls - 1)
 
-    line_copies = [[None] for _ in range(KPARTS)]
-    plane_copies = [[] for _ in range(KPARTS)]
-
-    def forward(i, part):
-        source = at(lax.rem(l + line - i, line), q)
-        for p in range(1, plane):
-            copy = remote(
-                spot(source, part),
-                spot(source, part),
-                gsend.at[part, i, p],
-                grecv.at[part, i, p],
-                at(l, lax.rem(q + p, plane)),
-            )
-            copy.start()
-            plane_copies[part].append(copy)
-
+    panel_copies = [[] for _ in range(KPARTS)]
     for part in range(KPARTS):
-        for i in range(1, line):
-            copy = remote(
-                spot(me, part),
-                spot(me, part),
-                gsend.at[part, i, 0],
-                grecv.at[part, i, 0],
-                at(lax.rem(l + i, line), q),
-            )
-            copy.start()
-            line_copies[part].append(copy)
-        forward(0, part)
+        for i in reversed(range(line)):
+            for p in range(plane):
+                if i == 0 and p == 0:
+                    continue
+                copy = remote(
+                    spot(me, part),
+                    spot(me, part),
+                    gsend.at[part, i, p],
+                    grecv.at[part, i, p],
+                    at(lax.rem(l + i, line), lax.rem(q + p, plane)),
+                )
+                copy.start()
+                panel_copies[part].append(copy)
 
     shell_pick = (iota((LANES, 1), 0) == over(iota((1, PIXC), 1), PIXC // NSHELL)).astype(
         F32
@@ -251,10 +238,6 @@
     per = quarter // step
     for i in range(4):
         loads[i].wait()
-        if i in (1, 2):
-            for s in range(1, line):
-                line_copies[i - 1][s].wait_recv()
-                forward(s, i - 1)
         prepare(i * per, (i + 1) * per)
 
     ids = jnp.broadcast_to(orient[...].astype(F32), (8, ORIENT)).astype(BF16)
@@ -283,7 +266,7 @@
 
     norm = jnp.zeros((total_rows, LANES), F32)
     for part in range(KPARTS):
-        for copy in plane_copies[part]:
+        for copy in panel_copies[part]:
             copy.wait_recv()
         whole = gathered[part]
         panel_real = dot(pick_real, whole)
@@ -478,7 +461,7 @@
             maps[0, h * rows : (h + 1) * rows, lanes] = value[:rows]
 
     for part in range(KPARTS):
-        for copy in line_copies[part][1:] + plane_copies[part]:
+        for copy in panel_copies[part]:
             copy.wait_send()
     for copy in stat_copies:
         copy.wait_send()

time: 50.6 us -> 55.3 us (1.093)
  Pallas kernels: 49.8 us -> 54.5 us
    pallas_call x1, Pallas kernels: 48.2 us -> 52.9 us  [on_device(): pl.pallas_call(functools.partial(kernel, dims), out_shape=(jax.ShapeDtype...]
where the time goes in v4:
time: 55.3 us; the launch traced here: 55.1 us
  Pallas kernels  54.5 us (99%)
  between operations  0.64 us (1%)
    pallas_call x1, Pallas kernels, on_device(): pl.pallas_call(functools.partial(kernel, dims), out_shape=(jax.ShapeDtype...  52.9 us
    pallas_call x1, Pallas kernels, on_device(): pl.pallas_call(write_out, out_shape=(jax.ShapeDtypeStruct(maps.shape, F32...  1.57 us

profile of v4, /device:TPU:0, one launch (start us, length us, event | category | flops | bytes accessed | tf_op | source)
XLA Modules:
  0.0 55.1 jit_solution(17339388897248632067)
XLA Ops:
  0.6 52.9 %shard_map.95 = (f32[1,16,2048]{2,1,0:T(8,128)}, f32[1,1024]{1,0:T(1,128)}) custom-call(bf16[1024,2048]{1,0:T(8,128)(2,1)} %particles.1, bf16[1,8,2048]{2,1,0:T(8,128)(2,1)} %panels.1, f32[1,32]{1,0:T(1,128)} %bitcast.9, s32[1,1024]{1,0:T(1,128)} %bitcast.6, s32[1,1024]{1,0:T(1,128)} %bitcast.7, s32[1,1024]{1,0:T(1,128)} %bitcast.8, s32[1,128]{1,0:T(1,128)} %bitcast.10, ...), custom_call_target="tpu_custom_call" | custom-call | tf_op jit(solution)/shard_map/pallas_call | solution.py:497
  53.6 1.6 %shard_map.96 = (f32[1,16,2048]{2,1,0:T(8,128)}, f32[1,1024]{1,0:T(1,128)}) custom-call(f32[1,16,2048]{2,1,0:T(8,128)} %get-tuple-element.6.maps, f32[1,1024]{1,0:T(1,128)} %get-tuple-element.7.evidence), custom_call_target="tpu_custom_call" | custom-call | tf_op jit(solution)/shard_map/pallas_call | solution.py:551
